TPU v7x, 512 devices: a whole 4x4x16 slice. The times are simulated.
512 devices in a mesh: dp: 64 (over x, z), mp: 8 (over y, core).
Axes of the slice: x: 4, y: 4, z: 16, core: 2. Of those that a mesh axis runs over, the one named last changes fastest.
Arguments:
- value_grads: bfloat16 [73728, 1024], P('dp', 'mp'), may hold values from -90 to 90
- activations: bfloat16 [73728, 5120], P(('dp', 'mp')), may hold values from -90 to 90
- block_moment: float32 [1032], replicated, may hold values from 368640 to 36864000
- first_moment: float32 [8, 5184, 128], P('mp', 'dp'), may hold values from -32768 to 32768
Outputs:
- update: float32 [8, 5184, 128], P('mp', 'dp')
All inputs are finite; a program needn't handle non-finite values.
Results may differ from a plain program's by a relative error of at most 0.0003.
Values may be sent and summed in bfloat16 or wider, within the bound.
A program may use at most 64 MiB of HBM per device.

v0:
```python
import jax
import jax.numpy as jnp
from jax import lax
from jax.sharding import PartitionSpec as P

beta_one = 0.9
beta_two = 0.95
bias_one = 1.0 - 0.9**10
bias_two = 1.0 - 0.95**10
epsilon = 1e-08


def padded(x, sides, width):
    for axis, dim in sides:
        devices, length = (lax.axis_size(axis), x.shape[dim])
        up = [(i, (i + 1) % devices) for i in range(devices - 1)]
        down = [(j, i) for i, j in up]
        last = lax.slice_in_dim(x, length - width, length, axis=dim)
        first = lax.slice_in_dim(x, 0, width, axis=dim)
        before = lax.ppermute(last, axis, up)
        after = lax.ppermute(first, axis, down)
        x = jnp.concatenate([before, x, after], axis=dim)
    return x


def block_index(position, head_size, model_width, used_len, sentinel):
    inner = jnp.maximum(position - head_size, 0) // model_width + 1
    return jnp.where(position < head_size, 0, jnp.where(position < used_len, inner, sentinel))


def body(value_grads, activations, block_moment, first_moment):
    head_size = value_grads.shape[1]
    model_width = activations.shape[1]
    unit_count = head_size * lax.axis_size("mp")
    part_rows = first_moment.shape[1]
    part_len = part_rows * 128
    total_rows = part_rows * lax.axis_size("dp")
    used_len = head_size + head_size * model_width
    sentinel = head_size + 1
    table_len = block_moment.shape[0]
    slot_count = part_len // model_width + 2
    head_index = lax.axis_index("mp")
    part_index = lax.axis_index("dp")
    weight_grad = lax.dot_general(
        value_grads,
        lax.all_gather(activations, "mp", axis=0, tiled=True),
        (((0,), (0,)), ((), ())),
        preferred_element_type=jnp.float32,
    )
    bias_grad = jnp.sum(value_grads, axis=0, dtype=jnp.float32)
    padding = jnp.zeros((total_rows * 128 - used_len,), jnp.float32)
    flat_grad = jnp.concatenate([bias_grad, weight_grad.reshape(-1), padding]).reshape(
        total_rows, 128
    )
    base = part_index * part_len
    position = base + jnp.arange(part_len, dtype=jnp.int32)
    first_block = block_index(base, head_size, model_width, used_len, sentinel)
    slot_ids = jnp.arange(slot_count, dtype=jnp.int32)
    slot_block = first_block + slot_ids
    element_slot = block_index(position, head_size, model_width, used_len, sentinel) - first_block
    slot_match = element_slot[:, None] == slot_ids[None, :]
    table_ids = jnp.where(
        slot_block == 0,
        unit_count + head_index,
        jnp.where(slot_block <= head_size, head_index * head_size + slot_block - 1, -1),
    )
    table_match = table_ids[:, None] == jnp.arange(table_len, dtype=jnp.int32)[None, :]
    part_grad = lax.psum_scatter(flat_grad, "dp", scatter_dimension=0, tiled=True).reshape(-1)
    squares = part_grad * part_grad
    partials = jnp.sum(jnp.where(slot_match, squares[:, None], 0.0), axis=0)
    last_block = block_index(base + part_len - 1, head_size, model_width, used_len, sentinel)
    last_slot = slot_ids == last_block - first_block
    head_part = partials[0]
    tail_part = jnp.sum(jnp.where(last_slot, partials, 0.0))
    edges = padded(jnp.stack([head_part, tail_part]), (("dp", 0),), 1)
    before = block_index(base - 1, head_size, model_width, used_len, sentinel)
    after = block_index(base + part_len, head_size, model_width, used_len, sentinel)
    join_left = (base > 0) & (before == first_block) & (first_block < sentinel)
    join_right = (after == last_block) & (last_block < sentinel)
    completed = partials + jnp.where((slot_ids == 0) & join_left, edges[0], 0.0)
    slot_totals = completed + jnp.where(last_slot & join_right, edges[3], 0.0)
    block_sizes = jnp.where(slot_block == 0, float(head_size), float(model_width))
    old_moment = jnp.sum(jnp.where(table_match, block_moment[None, :], 0.0), axis=1)
    slot_moment = beta_two * old_moment + (1.0 - beta_two) * (slot_totals / block_sizes)
    moment_field = jnp.sum(jnp.where(slot_match, slot_moment[None, :], 0.0), axis=1)
    valid = position < used_len
    momentum = beta_one * first_moment.reshape(-1) + (1.0 - beta_one) * part_grad
    step_dir = jnp.where(
        valid, momentum / bias_one / (jnp.sqrt(moment_field / bias_two) + epsilon), 0.0
    )
    return step_dir.reshape(first_moment.shape)


def solution(mesh):
    return jax.shard_map(
        body,
        mesh=mesh,
        in_specs=(P("dp", "mp"), P(("dp", "mp"), None), P(), P("mp", "dp", None)),
        out_specs=P("mp", "dp", None),
        check_vma=False,
    )
```

profile of v0, /device:TPU:4, one launch (start us, length us, event | category | flops | bytes accessed | tf_op | source)
XLA Modules:
  0.0 341.0 jit_solution(7200127885950705412)
XLA Ops:
  6.5 0.7 all-gather.2.cloned.1.call-update
  7.3 1.1 convert_reduce_fusion
  8.4 0.1 fusion.4
  8.5 77.2 %all-gather.2.cloned.1.call-done = bf16[1152,5120]{1,0:T(8,128)(2,1)} async-done(((bf16[144,5120]{1,0:T(8,128)(2,1)}), bf16[1152,5120]{1,0:T(8,128)(2,1)}) %all-gather.2.cloned.1.call-update) | async-done | bytes 11796496 | tf_op jit(solution)/shard_map/all_gather | solution.py:46
  85.7 6.4 %convolution_bitcast_fusion = f32[16,40,8,128]{3,2,1,0:T(8,128)S(1)} fusion(bf16[1152,128]{1,0:T(8,128)(2,1)} %param.4, bf16[1152,5120]{1,0:T(8,128)(2,1)} %all-gather.2.cloned.1.call-done), kind=kOutput, calls=%fused_computation.1 | convolution fusion | flops 1509949440 | bytes 14712832 | tf_op jit(solution)/shard_map/dot_general | solution.py:44
  92.0 0.5 copy.9
  92.5 0.2 maximum_bitcast_fusion
  92.7 142.6 %fusion = f32[96,128]{1,0:T(8,128)S(1)} fusion(f32[5184,128]{1,0:T(8,128)S(1)} %maximum_bitcast_fusion), kind=kCustom, calls=%all-reduce-scatter | all-reduce-scatter fusion | flops 786433 | bytes 2705408
  235.3 1.9 collective-permute-start.10
  237.3 2.5 collective-permute-start.2
  239.8 5.0 %collective-permute-start.3 = (f32[96,128]{1,0:T(8,128)S(1)}, f32[96,128]{1,0:T(8,128)S(1)}, u32[]{:S(2)}, u32[]{:S(2)}) collective-permute-start(f32[96,128]{1,0:T(8,128)S(1)} %fusion), channel_id=1, source_target_pairs={{0,16},{8,24},{16,32},{24,40},{32,48},{40,56},{48,64},{56,72},{64,... | collective-permute-start | bytes 147464
  244.8 6.4 %collective-permute-start.4 = (f32[96,128]{1,0:T(8,128)S(1)}, f32[96,128]{1,0:T(8,128)S(1)}, u32[]{:S(2)}, u32[]{:S(2)}) collective-permute-start(f32[96,128]{1,0:T(8,128)S(1)} %fusion), channel_id=1, source_target_pairs={{0,24},{8,32},{16,40},{24,48},{32,56},{40,64},{48,72},{56,80},{64,... | collective-permute-start | bytes 147464
  251.2 17.3 %collective-permute-start.11 = (f32[81,128]{1,0:T(8,128)S(1)}, f32[81,128]{1,0:T(8,128)S(1)}, u32[]{:S(2)}, u32[]{:S(2)}) collective-permute-start(f32[81,128]{1,0:T(8,128)S(1)} %slice.4), channel_id=1, source_target_pairs={{0,80},{8,88},{16,96},{24,104},{32,112},{40,120},{48,128},{56,136}... | collective-permute-start | bytes 124424
  268.5 1.7 collective-permute-done.11
  270.2 11.7 %collective-permute-start.5 = (f32[96,128]{1,0:T(8,128)S(1)}, f32[96,128]{1,0:T(8,128)S(1)}, u32[]{:S(2)}, u32[]{:S(2)}) collective-permute-start(f32[96,128]{1,0:T(8,128)S(1)} %fusion), channel_id=1, source_target_pairs={{0,32},{8,40},{16,48},{24,56},{32,64},{40,72},{48,80},{56,88},{64,... | collective-permute-start | bytes 147464
  282.0 5.4 %collective-permute-start.6 = (f32[96,128]{1,0:T(8,128)S(1)}, f32[96,128]{1,0:T(8,128)S(1)}, u32[]{:S(2)}, u32[]{:S(2)}) collective-permute-start(f32[96,128]{1,0:T(8,128)S(1)} %fusion), channel_id=1, source_target_pairs={{0,40},{8,48},{16,56},{24,64},{32,72},{40,80},{48,88},{56,96},{64,... | collective-permute-start | bytes 147464
  287.4 11.5 %collective-permute-start.7 = (f32[96,128]{1,0:T(8,128)S(1)}, f32[96,128]{1,0:T(8,128)S(1)}, u32[]{:S(2)}, u32[]{:S(2)}) collective-permute-start(f32[96,128]{1,0:T(8,128)S(1)} %fusion), channel_id=1, source_target_pairs={{0,48},{8,56},{16,64},{24,72},{32,80},{40,88},{48,96},{56,104},{64... | collective-permute-start | bytes 147464
  298.9 5.6 %collective-permute-start.8 = (f32[96,128]{1,0:T(8,128)S(1)}, f32[96,128]{1,0:T(8,128)S(1)}, u32[]{:S(2)}, u32[]{:S(2)}) collective-permute-start(f32[96,128]{1,0:T(8,128)S(1)} %fusion), channel_id=1, source_target_pairs={{0,56},{8,64},{16,72},{24,80},{32,88},{40,96},{48,104},{56,112},{6... | collective-permute-start | bytes 147464
  304.5 2.9 collective-permute-start.9
  307.4 0.2 select_reduce_fusion.2
  307.6 1.3 dynamic-slice.4
  309.6 4.3 %collective-permute-done.8 = f32[96,128]{1,0:T(8,128)S(1)} collective-permute-done((f32[96,128]{1,0:T(8,128)S(1)}, f32[96,128]{1,0:T(8,128)S(1)}, u32[]{:S(2)}, u32[]{:S(2)}) %collective-permute-start.8) | collective-permute-done | bytes 49184
  313.8 6.2 %collective-permute-done.9 = f32[96,128]{1,0:T(8,128)S(1)} collective-permute-done((f32[96,128]{1,0:T(8,128)S(1)}, f32[96,128]{1,0:T(8,128)S(1)}, u32[]{:S(2)}, u32[]{:S(2)}) %collective-permute-start.9) | collective-permute-done | bytes 49184
  320.1 1.8 concatenate.4
  321.9 0.2 select_reduce_fusion.1
  322.1 0.6 fusion.12
  322.7 3.8 %collective-permute-start = (f32[1]{0:T(128)}, f32[1]{0:T(128)}, u32[]{:S(2)}, u32[]{:S(2)}) collective-permute-start(f32[1]{0:T(128)} %bitcast.3), channel_id=1, source_target_pairs={{0,8},{8,16},{16,24},{24,32},{32,40},{40,48},{48,56},{56,64},{64,7... | collective-permute-start | bytes 20 | tf_op jit(solution)/shard_map/ppermute | solution.py:20
  326.5 4.2 %collective-permute-start.1 = (f32[1]{0:T(128)S(1)}, f32[1]{0:T(128)}, u32[]{:S(2)}, u32[]{:S(2)}) collective-permute-start(f32[1]{0:T(128)S(1)} %bitcast.27), channel_id=1, source_target_pairs={{8,0},{16,8},{24,16},{32,24},{40,32},{48,40},{56,48},{64,56},{72,6... | collective-permute-start | bytes 20 | tf_op jit(solution)/shard_map/ppermute | solution.py:21
  330.7 1.3 collective-permute-done.1
  332.0 1.3 multiply_add_fusion
  333.3 0.2 select_reduce_fusion
  333.5 0.7 copy.8
  (18 shorter events, 0.1 us)
Async XLA Ops:
  6.5 79.1 %all-gather.2.cloned.1.call-start = ((), (), s32[]{:S(2)}) async-start(), calls=%async_computation | async-start | bytes 13271040 | tf_op jit(solution)/shard_map/all_gather | solution.py:46
  92.7 214.7 %copy-start.1 = (f32[1032]{0:T(1024)S(1)}, f32[1032]{0:T(1024)}, u32[]{:S(2)}) copy-start(f32[1032]{0:T(1024)} %param.6) | copy-start | bytes 12388
  92.7 240.7 %copy-start = (f32[1,81,128]{2,0,1:T(1,128)S(1)}, f32[1,81,128]{2,0,1:T(1,128)}, u32[]{:S(2)}) copy-start(f32[1,81,128]{2,0,1:T(1,128)} %param.7) | copy-start | bytes 124420
  235.3 46.6 %collective-permute-start.10 = (f32[96,128]{1,0:T(8,128)S(1)}, f32[96,128]{1,0:T(8,128)S(1)}, u32[]{:S(2)}, u32[]{:S(2)}) collective-permute-start(f32[96,128]{1,0:T(8,128)S(1)} %fusion), channel_id=1, source_target_pairs={{0,72},{8,80},{16,88},{24,96},{32,104},{40,112},{48,120},{56,128},... | collective-permute-start | bytes 147464
  237.3 50.1 %collective-permute-start.2 = (f32[96,128]{1,0:T(8,128)S(1)}, f32[96,128]{1,0:T(8,128)S(1)}, u32[]{:S(2)}, u32[]{:S(2)}) collective-permute-start(f32[96,128]{1,0:T(8,128)S(1)} %fusion), channel_id=1, source_target_pairs={{0,8},{8,16},{16,24},{24,32},{32,40},{40,48},{48,56},{56,64},{64,7... | collective-permute-start | bytes 147464
  239.8 59.0 %collective-permute-start.3 = (f32[96,128]{1,0:T(8,128)S(1)}, f32[96,128]{1,0:T(8,128)S(1)}, u32[]{:S(2)}, u32[]{:S(2)}) collective-permute-start(f32[96,128]{1,0:T(8,128)S(1)} %fusion), channel_id=1, source_target_pairs={{0,16},{8,24},{16,32},{24,40},{32,48},{40,56},{48,64},{56,72},{64,... | collective-permute-start | bytes 147464
  244.8 59.6 %collective-permute-start.4 = (f32[96,128]{1,0:T(8,128)S(1)}, f32[96,128]{1,0:T(8,128)S(1)}, u32[]{:S(2)}, u32[]{:S(2)}) collective-permute-start(f32[96,128]{1,0:T(8,128)S(1)} %fusion), channel_id=1, source_target_pairs={{0,24},{8,32},{16,40},{24,48},{32,56},{40,64},{48,72},{56,80},{64,... | collective-permute-start | bytes 147464
  251.2 19.0 %collective-permute-start.11 = (f32[81,128]{1,0:T(8,128)S(1)}, f32[81,128]{1,0:T(8,128)S(1)}, u32[]{:S(2)}, u32[]{:S(2)}) collective-permute-start(f32[81,128]{1,0:T(8,128)S(1)} %slice.4), channel_id=1, source_target_pairs={{0,80},{8,88},{16,96},{24,104},{32,112},{40,120},{48,128},{56,136}... | collective-permute-start | bytes 124424
  270.2 39.4 %collective-permute-start.5 = (f32[96,128]{1,0:T(8,128)S(1)}, f32[96,128]{1,0:T(8,128)S(1)}, u32[]{:S(2)}, u32[]{:S(2)}) collective-permute-start(f32[96,128]{1,0:T(8,128)S(1)} %fusion), channel_id=1, source_target_pairs={{0,32},{8,40},{16,48},{24,56},{32,64},{40,72},{48,80},{56,88},{64,... | collective-permute-start | bytes 147464
  282.0 27.6 %collective-permute-start.6 = (f32[96,128]{1,0:T(8,128)S(1)}, f32[96,128]{1,0:T(8,128)S(1)}, u32[]{:S(2)}, u32[]{:S(2)}) collective-permute-start(f32[96,128]{1,0:T(8,128)S(1)} %fusion), channel_id=1, source_target_pairs={{0,40},{8,48},{16,56},{24,64},{32,72},{40,80},{48,88},{56,96},{64,... | collective-permute-start | bytes 147464
  287.4 22.2 %collective-permute-start.7 = (f32[96,128]{1,0:T(8,128)S(1)}, f32[96,128]{1,0:T(8,128)S(1)}, u32[]{:S(2)}, u32[]{:S(2)}) collective-permute-start(f32[96,128]{1,0:T(8,128)S(1)} %fusion), channel_id=1, source_target_pairs={{0,48},{8,56},{16,64},{24,72},{32,80},{40,88},{48,96},{56,104},{64... | collective-permute-start | bytes 147464
  298.9 15.0 %collective-permute-start.8 = (f32[96,128]{1,0:T(8,128)S(1)}, f32[96,128]{1,0:T(8,128)S(1)}, u32[]{:S(2)}, u32[]{:S(2)}) collective-permute-start(f32[96,128]{1,0:T(8,128)S(1)} %fusion), channel_id=1, source_target_pairs={{0,56},{8,64},{16,72},{24,80},{32,88},{40,96},{48,104},{56,112},{6... | collective-permute-start | bytes 147464
  304.5 15.6 %collective-permute-start.9 = (f32[96,128]{1,0:T(8,128)S(1)}, f32[96,128]{1,0:T(8,128)S(1)}, u32[]{:S(2)}, u32[]{:S(2)}) collective-permute-start(f32[96,128]{1,0:T(8,128)S(1)} %fusion), channel_id=1, source_target_pairs={{0,64},{8,72},{16,80},{24,88},{32,96},{40,104},{48,112},{56,120},{... | collective-permute-start | bytes 147464
  322.7 8.1 %collective-permute-start = (f32[1]{0:T(128)}, f32[1]{0:T(128)}, u32[]{:S(2)}, u32[]{:S(2)}) collective-permute-start(f32[1]{0:T(128)} %bitcast.3), channel_id=1, source_target_pairs={{0,8},{8,16},{16,24},{24,32},{32,40},{40,48},{48,56},{56,64},{64,7... | collective-permute-start | bytes 20 | tf_op jit(solution)/shard_map/ppermute | solution.py:20
  326.5 5.5 %collective-permute-start.1 = (f32[1]{0:T(128)S(1)}, f32[1]{0:T(128)}, u32[]{:S(2)}, u32[]{:S(2)}) collective-permute-start(f32[1]{0:T(128)S(1)} %bitcast.27), channel_id=1, source_target_pairs={{8,0},{16,8},{24,16},{32,24},{40,32},{48,40},{56,48},{64,56},{72,6... | collective-permute-start | bytes 20 | tf_op jit(solution)/shard_map/ppermute | solution.py:21
Sparse Core Ops, SparseCore 0:
  9.5 76.1 all-gather.1
where the time goes:
time: 342 us; the launch traced here: 341 us
  blocking collectives  143 us (42%)
  waiting for transfers between devices  91.4 us (27%)
  starting transfers between devices  78.3 us (23%)
  between operations  14.4 us (4%)
  matrix products  6.36 us (2%)
  local copies, waits for them, and re-layouts  4.17 us (1%)
  other arithmetic  3.87 us (1%)
    unnamed x1, blocking collectives  143 us
    all_gather x1, waiting for transfers between devices, body(): lax.all_gather(activations, 'mp', axis=0, tiled=True)  77.2 us
    unnamed x10, starting transfers between devices  70.2 us
    unnamed x11, waiting for transfers between devices  12.9 us
  transfers between devices with their start and end apart: 13, of which 5 were waited for; matrix products, arithmetic and copies ran while one was open for 1% of the time, Pallas kernels for 0%

commit v1 on v0

v1 whole, which is shorter than its diff:
```python
import functools

import jax
import jax.numpy as jnp
import numpy as np
from jax import lax
from jax.experimental import pallas as pl
from jax.experimental.pallas import tpu as pltpu
from jax.sharding import PartitionSpec as P

MESH = pl.DeviceIdType.MESH

beta_one = 0.9
beta_two = 0.95
bias_one = 1.0 - 0.9**10
bias_two = 1.0 - 0.95**10
epsilon = 1e-08

NX, NZ, NY, NC = 4, 16, 4, 2
NDP, NMP = NX * NZ, NY * NC
LANES = 128
HEAD = 128
TOK = 144
TOKENS = TOK * NMP
WIDTH = 5120
SLICE = WIDTH // NMP
CH = SLICE // LANES
ROWS_P = 81
USED_ROWS = 1 + HEAD * WIDTH // LANES
UNIT_ROWS = WIDTH // LANES


def unit_order():
    order = np.zeros((HEAD, HEAD), np.float32)
    for e in range(2):
        for x in range(NX):
            for zl in range(4):
                for zh in range(4):
                    q = x * 16 + zl * 4 + zh
                    p = x * 16 + zh * 4 + zl
                    order[e * 64 + q, 2 * p + e] = 1.0
    return order


def kernel(
    perm_ref, vg_ref, act_ref, block_ref, first_ref, out_ref,
    vt, a_buf, r_buf, x1, s1, x2, near_out, near_in, far_out, far_in, g_buf, g_in, rows, denom,
    bias_out, bias_x, bias_n, bias_f,
    v_send, v_recv, w_send, a_send, a_recv, x1_send, x1_recv, x2_send, x2_recv,
    n_send, n_recv, f_send, f_recv, g_send, g_recv, b_send, b_recv,
):
    dp, mp = lax.axis_index("dp"), lax.axis_index("mp")
    x, z = dp // NZ, dp % NZ
    zh, zl = z // 4, z % 4
    y, c = mp // NC, mp % NC

    def at(px=None, pz=None, m=None, p=None):
        if p is None:
            p = (x if px is None else px) * NZ + (z if pz is None else pz)
        return {"dp": p, "mp": mp if m is None else m}

    def remote(src, dst, send, recv, device):
        return pltpu.make_async_remote_copy(
            src_ref=src, dst_ref=dst, send_sem=send, recv_sem=recv, device_id=device, device_id_type=MESH
        )

    mp_others = [(mp + k) % NMP for k in range(1, NMP)]
    y_others = [(y + k) % NY for k in range(1, NY)]
    x_others = [(x + k) % NX for k in range(1, NX)]
    zl_others = [(zl + k) % 4 for k in range(1, 4)]
    zh_others = [(zh + k) % 4 for k in range(1, 4)]
    before, after = (dp + NDP - 1) % NDP, (dp + 1) % NDP
    odd = x % 2
    pair = x + 1 - 2 * odd
    cross = (x + NX - 1 + 2 * odd) % NX

    def cross_of(v):
        return (v + NX - 1 + 2 * (v % 2)) % NX

    def pair_of(v):
        return v + 1 - 2 * (v % 2)

    with jax.named_scope("entry"):
        barrier = pltpu.get_barrier_semaphore()
        partners = [at(m=m) for m in mp_others]
        partners += [at(px=v) for v in x_others]
        partners += [at(pz=zh * 4 + v) for v in zl_others]
        partners += [at(pz=v * 4 + zl) for v in zh_others]
        partners += [at(p=p, m=m) for p in (before, after) for m in range(NMP)]
        for partner in partners:
            pl.semaphore_signal(barrier, inc=1, device_id=partner, device_id_type=MESH)
        for j in range(CH):
            columns = pl.ds(pl.multiple_of(mp * SLICE + j * LANES, LANES), LANES)
            own = pl.ds(pl.multiple_of(mp * TOK, TOK), TOK)
            pltpu.make_async_copy(act_ref.at[:, columns], a_buf.at[j, own], a_recv.at[j]).start()
    with jax.named_scope("turn"):
        vt[mp] = lax.dot_general(
            perm_ref[...], vg_ref[...], (((1,), (1,)), ((), ())), preferred_element_type=jnp.float32
        ).astype(jnp.bfloat16)
        bias = jnp.sum(vg_ref[...].astype(jnp.float32), axis=0, keepdims=True)
        bias_out[0] = jnp.broadcast_to(bias, (8, LANES))
    with jax.named_scope("barrier"):
        pl.semaphore_wait(barrier, len(partners))

    def v_copy(v, slot):
        return remote(vt.at[slot], vt.at[slot], v_send, v_recv.at[slot], at(m=v * NC + c))

    def w_copy(slot):
        return remote(vt.at[slot], vt.at[slot], w_send, v_recv.at[slot], at(m=y * NC + 1 - c))

    def a_copy(j, m):
        columns = pl.ds(pl.multiple_of(m * SLICE + j * LANES, LANES), LANES)
        own = pl.ds(pl.multiple_of(mp * TOK, TOK), TOK)
        return remote(act_ref.at[:, columns], a_buf.at[j, own], a_send.at[j], a_recv.at[j], at(m=m))

    with jax.named_scope("send"):
        for v in y_others:
            v_copy(v, mp).start()
        w_copy(mp).start()
        for j in range(CH):
            for m in mp_others:
                a_copy(j, m).start()

        @pl.when(x != 0)
        def _():
            remote(bias_out.at[0], bias_x.at[x], b_send.at[0], b_recv.at[0], at(px=0)).start()

    with jax.named_scope("forward"):
        for v in y_others:
            slot = v * NC + c
            v_copy(y, slot).wait_recv()
            w_copy(slot).start()
        for v in range(NY):
            w_copy(v * NC + 1 - c).wait_recv()

    def first_of(half):
        return (pair, cross_of(pair)) if half == 0 else (cross, pair_of(cross))

    def second_of(half):
        return cross if half == 0 else pair

    def block(b):
        return pl.ds(pl.multiple_of(b * 128, 128), 128)

    def x1_copies(j, half):
        to, other = first_of(half)
        return [
            remote(r_buf.at[j, half, block(b)], x1.at[j, half, k], x1_send.at[j, half], x1_recv.at[j, half, k], at(px=to))
            for k, b in ((1, other), (0, to))
        ]

    def x2_copy(j, half):
        return remote(s1.at[j, half], x2.at[j, half], x2_send.at[j, half], x2_recv.at[j, half], at(px=second_of(half)))

    def near_copy(j, v):
        return remote(near_out.at[j, v], near_in.at[j, zl], n_send.at[j], n_recv.at[j], at(pz=zh * 4 + v))

    def far_copy(j, v):
        return remote(far_out.at[j, v], far_in.at[j, zh], f_send.at[j], f_recv.at[j], at(pz=v * 4 + zl))

    def stage_mul(j):
        with jax.named_scope("mul"):
            pltpu.make_async_copy(a_buf.at[j], a_buf.at[j], a_recv.at[j]).wait()
            for half in range(2):
                for v in range(NY):
                    res = jnp.dot(vt[v * NC + half], a_buf[j], preferred_element_type=jnp.float32)
                    for e in range(2):
                        r_buf[j, half, pl.ds(v * 2 + e, 64, stride=8), :] = res[e * 64 : (e + 1) * 64]
                for copy in x1_copies(j, half):
                    copy.start()

    def stage_x1(j):
        with jax.named_scope("x1"):
            for half in range(2):
                copies = x1_copies(j, half)
                copies[0].wait_recv()
                s1[j, half] = r_buf[j, half, block(second_of(half))] + x1[j, half, 1]
                x2_copy(j, half).start()
            for half in range(2):
                x1_copies(j, half)[1].wait_recv()

    def stage_x2(j):
        with jax.named_scope("x2"):
            for half in range(2):
                x2_copy(j, half).wait_recv()
                total = r_buf[j, half, block(x)] + x1[j, half, 0] + x2[j, half]
                for v in range(4):
                    near_out[j, v, half * 32 : half * 32 + 32] = total[v * 32 : v * 32 + 32]
            for v in zl_others:
                near_copy(j, v).start()
            near_in[j, zl] = near_out[j, zl]

    def stage_near(j):
        with jax.named_scope("near"):
            pltpu.make_async_copy(near_in.at[j, pl.ds(0, 3)], near_in.at[j, pl.ds(0, 3)], n_recv.at[j]).wait()
            total = near_in[j, 0] + near_in[j, 1] + near_in[j, 2] + near_in[j, 3]
            for v in range(4):
                for half in range(2):
                    far_out[j, v, half * 8 : half * 8 + 8] = total[half * 32 + v * 8 : half * 32 + v * 8 + 8]
            for v in zh_others:
                far_copy(j, v).start()
            far_in[j, zh] = far_out[j, zh]

    def stage_far(j):
        with jax.named_scope("far"):
            pltpu.make_async_copy(far_in.at[j, pl.ds(0, 3)], far_in.at[j, pl.ds(0, 3)], f_recv.at[j]).wait()
            total = far_in[j, 0] + far_in[j, 1] + far_in[j, 2] + far_in[j, 3]
            for half in range(2):
                g_buf[pl.ds(half * 64 + j, 8, stride=8), :] = total[half * 8 : half * 8 + 8]

    def bias_stage(k):
        if k == 0:

            @pl.when(x == 0)
            def _():
                pltpu.make_async_copy(bias_x.at[pl.ds(1, 3)], bias_x.at[pl.ds(1, 3)], b_recv.at[0]).wait()
                bias_out[1] = bias_out[0] + bias_x[1] + bias_x[2] + bias_x[3]

                @pl.when(zl != 0)
                def _():
                    remote(bias_out.at[1], bias_n.at[zl], b_send.at[1], b_recv.at[1], at(pz=zh * 4)).start()

        elif k == 1:

            @pl.when((x == 0) & (zl == 0))
            def _():
                pltpu.make_async_copy(bias_n.at[pl.ds(1, 3)], bias_n.at[pl.ds(1, 3)], b_recv.at[1]).wait()
                bias_out[2] = bias_out[1] + bias_n[1] + bias_n[2] + bias_n[3]

                @pl.when(zh != 0)
                def _():
                    remote(bias_out.at[2], bias_f.at[zh], b_send.at[2], b_recv.at[2], at(pz=0)).start()

        else:

            @pl.when(dp == 0)
            def _():
                pltpu.make_async_copy(bias_f.at[pl.ds(1, 3)], bias_f.at[pl.ds(1, 3)], b_recv.at[2]).wait()
                rows[0:8] = bias_out[2] + bias_f[1] + bias_f[2] + bias_f[3]

    rows[0:8] = jnp.zeros((8, LANES), jnp.float32)
    stages = [stage_mul, stage_x1, stage_x2, stage_near, stage_far]
    for step in range(CH + len(stages) - 1):
        for lag, stage in enumerate(stages):
            if 0 <= step - lag < CH:
                stage(step - lag)
        if step < 3:
            bias_stage(step)

    def g_copy(k, m):
        src = g_buf.at[pl.ds(pl.multiple_of(((m % NC) * NY + m // NC) * 16, 16), 16)]
        dst = g_in.at[k, pl.ds(pl.multiple_of(mp * 16, 16), 16)]
        return remote(src, dst, g_send, g_recv.at[k], at(p=dp if k == 0 else before, m=m))

    with jax.named_scope("heads"):
        for m in mp_others:
            g_copy(0, m).start()
        for k in range(NMP):
            g_copy(1, (mp + k) % NMP).start()
        own = pl.ds(pl.multiple_of(mp * 16, 16), 16)
        g_in[0, own] = g_buf[pl.ds(pl.multiple_of((c * NY + y) * 16, 16), 16)]
        pltpu.make_async_copy(g_in.at[0, pl.ds(0, 112)], g_in.at[0, pl.ds(0, 112)], g_recv.at[0]).wait()
        pltpu.make_async_copy(g_in.at[1], g_in.at[1], g_recv.at[1]).wait()

    with jax.named_scope("update"):
        for k in range(2):
            for m in range(NMP):
                for e in range(2):
                    start = 8 + k * 80 + e * 40 + CH * m
                    rows[start : start + CH] = g_in[k, m * 16 + e * 8 : m * 16 + e * 8 + CH]
        head_total = jnp.sum(rows[0:8] * rows[0:8]) / 8.0
        head_moment = beta_two * block_ref[NMP * HEAD + mp] + (1.0 - beta_two) * (head_total / HEAD)
        denom[0:8] = jnp.full((8, LANES), head_moment, jnp.float32)
        for k in range(4):
            unit = rows[8 + k * 40 : 48 + k * 40]
            unit_moment = beta_two * block_ref[mp * HEAD + 2 * dp + k] + (1.0 - beta_two) * (
                jnp.sum(unit * unit) / WIDTH
            )
            denom[8 + k * 40 : 48 + k * 40] = jnp.full((40, LANES), unit_moment, jnp.float32)
        grad = rows[pl.ds(dp + 7, ROWS_P), :]
        moment = denom[pl.ds(dp + 7, ROWS_P), :]
        momentum = beta_one * first_ref[0] + (1.0 - beta_one) * grad
        step_dir = momentum / bias_one / (jnp.sqrt(moment / bias_two) + epsilon)
        position = dp * ROWS_P + lax.broadcasted_iota(jnp.int32, (ROWS_P, LANES), 0)
        out_ref[0] = jnp.where(position < USED_ROWS, step_dir, 0.0)

    with jax.named_scope("drain"):
        for v in y_others:
            v_copy(v, mp).wait_send()
        for v in range(NY):
            w_copy(v * NC + c).wait_send()
        for j in range(CH):
            for m in mp_others:
                a_copy(j, m).wait_send()
            for half in range(2):
                for copy in x1_copies(j, half):
                    copy.wait_send()
                x2_copy(j, half).wait_send()
            for v in zl_others:
                near_copy(j, v).wait_send()
            for v in zh_others:
                far_copy(j, v).wait_send()
        for m in mp_others:
            g_copy(0, m).wait_send()
        for m in range(NMP):
            g_copy(1, m).wait_send()

        @pl.when(x != 0)
        def _():
            remote(bias_out.at[0], bias_x.at[x], b_send.at[0], b_recv.at[0], at(px=0)).wait_send()

        @pl.when((x == 0) & (zl != 0))
        def _():
            remote(bias_out.at[1], bias_n.at[zl], b_send.at[1], b_recv.at[1], at(pz=zh * 4)).wait_send()

        @pl.when((x == 0) & (zl == 0) & (zh != 0))
        def _():
            remote(bias_out.at[2], bias_f.at[zh], b_send.at[2], b_recv.at[2], at(pz=0)).wait_send()


def body(value_grads, activations, block_moment, first_moment):
    f32, bf16 = jnp.float32, jnp.bfloat16
    dma = pltpu.SemaphoreType.DMA
    vmem = pl.BlockSpec(memory_space=pltpu.VMEM)
    return pl.pallas_call(
        kernel,
        out_shape=jax.ShapeDtypeStruct(first_moment.shape, f32),
        in_specs=[
            vmem,
            vmem,
            pl.BlockSpec(memory_space=pl.ANY),
            pl.BlockSpec(memory_space=pltpu.SMEM),
            vmem,
        ],
        out_specs=vmem,
        scratch_shapes=[
            pltpu.VMEM((NMP, HEAD, TOKENS), bf16),
            pltpu.VMEM((CH, TOKENS, LANES), bf16),
            pltpu.VMEM((CH, 2, 512, LANES), f32),
            pltpu.VMEM((CH, 2, 2, 128, LANES), f32),
            pltpu.VMEM((CH, 2, 128, LANES), f32),
            pltpu.VMEM((CH, 2, 128, LANES), f32),
            pltpu.VMEM((CH, 4, 64, LANES), f32),
            pltpu.VMEM((CH, 4, 64, LANES), f32),
            pltpu.VMEM((CH, 4, 16, LANES), f32),
            pltpu.VMEM((CH, 4, 16, LANES), f32),
            pltpu.VMEM((128, LANES), f32),
            pltpu.VMEM((2, 128, LANES), f32),
            pltpu.VMEM((168, LANES), f32),
            pltpu.VMEM((168, LANES), f32),
            pltpu.VMEM((3, 8, LANES), f32),
            pltpu.VMEM((4, 8, LANES), f32),
            pltpu.VMEM((4, 8, LANES), f32),
            pltpu.VMEM((4, 8, LANES), f32),
            dma, dma((NMP,)), dma, dma((CH,)), dma((CH,)),
            dma((CH, 2)), dma((CH, 2, 2)), dma((CH, 2)), dma((CH, 2)),
            dma((CH,)), dma((CH,)), dma((CH,)), dma((CH,)),
            dma, dma((2,)), dma((3,)), dma((3,)),
        ],
        compiler_params=pltpu.CompilerParams(
            collective_id=0, has_side_effects=True, vmem_limit_bytes=48 << 20
        ),
        name="gradient_step",
    )(jnp.asarray(unit_order(), bf16), value_grads, activations, block_moment, first_moment)


def solution(mesh):
    return jax.shard_map(
        body,
        mesh=mesh,
        in_specs=(P("dp", "mp"), P(("dp", "mp"), None), P(), P("mp", "dp", None)),
        out_specs=P("mp", "dp", None),
        check_vma=False,
    )
```

time: 342 us -> 89.6 us (0.26)
  the two profiles are of different devices: /device:TPU:4 before, /device:TPU:1 now
where the time goes in v1:
time: 89.6 us; the launch traced here: 89.3 us
  Pallas kernels  84.1 us (94%)
  local copies, waits for them, and re-layouts  5.23 us (6%)
    pallas_call x1, Pallas kernels, body(): pl.pallas_call(kernel, out_shape=jax.ShapeDtypeStruct(first_moment.shape,...  84.1 us
    unnamed x9, local copies, waits for them, and re-layouts  4.57 us

profile of v1, /device:TPU:1, one launch (start us, length us, event | category | flops | bytes accessed | tf_op | source)
XLA Modules:
  0.0 89.3 jit_solution(5523376416738541165)
XLA Ops:
  0.0 0.8 copy.6.first_ref
  0.8 0.0 copy-start
  0.8 1.4 %copy-done = bf16[144,5120]{1,0:T(8,128)(2,1)S(1)} copy-done((bf16[144,5120]{1,0:T(8,128)(2,1)S(1)}, bf16[144,5120]{1,0:T(8,128)(2,1)}, u32[]{:S(2)}) %copy-start) | copy-done | bytes 1474584
  2.2 0.0 copy-start.1
  2.2 1.0 %copy-done.1 = bf16[1152,128]{1,0:T(8,128)(2,1)S(1)} copy-done((bf16[1152,128]{1,0:T(8,128)(2,1)S(1)}, bf16[1152,128]{1,0:T(8,128)(2,1)}, u32[]{:S(2)}) %copy-start.1) | copy-done | bytes 294936
  3.1 0.0 copy-start.2
  3.1 0.8 copy-done.2
  3.9 0.0 copy-start.3
  3.9 0.7 copy-done.3
  4.6 84.1 %gradient_step.1 = f32[1,81,128]{2,1,0:T(8,128)S(1)} custom-call(bf16[128,128]{1,0:T(8,128)(2,1)S(1)} %copy-done.2, bf16[1152,128]{1,0:T(8,128)(2,1)S(1)} %copy-done.1, bf16[144,5120]{1,0:T(8,128)(2,1)S(1)} %copy-done, f32[1032]{0:T(1024)S(1)} %copy-done.3, f32[1,81,128]{2,1,0:T(8,128)S(1)} %copy.6.first_ref), custom_call_target="tpu_custom_call" | custom-call | tf_op jit(solution)/shard_map/gradient_step/pallas_call | solution.py:325
  88.6 0.7 copy.7
Async XLA Ops:
  0.8 1.4 %copy-start = (bf16[144,5120]{1,0:T(8,128)(2,1)S(1)}, bf16[144,5120]{1,0:T(8,128)(2,1)}, u32[]{:S(2)}) copy-start(bf16[144,5120]{1,0:T(8,128)(2,1)} %act_ref.1) | copy-start | bytes 4423684
  2.2 1.0 %copy-start.1 = (bf16[1152,128]{1,0:T(8,128)(2,1)S(1)}, bf16[1152,128]{1,0:T(8,128)(2,1)}, u32[]{:S(2)}) copy-start(bf16[1152,128]{1,0:T(8,128)(2,1)} %vg_ref.1) | copy-start | bytes 884740
  3.1 0.8 copy-start.2
  3.9 0.7 copy-start.3

commit v2 on v1

--- a/solution.py
+++ b/solution.py
@@ -2,7 +2,6 @@
 
 import jax
 import jax.numpy as jnp
-import numpy as np
 from jax import lax
 from jax.experimental import pallas as pl
 from jax.experimental.pallas import tpu as pltpu
@@ -31,21 +30,18 @@
 
 
 def unit_order():
-    order = np.zeros((HEAD, HEAD), np.float32)
-    for e in range(2):
-        for x in range(NX):
-            for zl in range(4):
-                for zh in range(4):
-                    q = x * 16 + zl * 4 + zh
-                    p = x * 16 + zh * 4 + zl
-                    order[e * 64 + q, 2 * p + e] = 1.0
-    return order
+    r = lax.broadcasted_iota(jnp.int32, (HEAD, HEAD), 0)
+    unit = lax.broadcasted_iota(jnp.int32, (HEAD, HEAD), 1)
+    e, q = r // 64, r % 64
+    p = (q // 16) * 16 + (q % 4) * 4 + (q // 4) % 4
+    return jnp.where(unit == 2 * p + e, 1.0, 0.0).astype(jnp.bfloat16)
 
 
 def kernel(
-    perm_ref, vg_ref, act_ref, block_ref, first_ref, out_ref,
+    vg_hbm, act_ref, block_hbm, first_hbm, out_hbm,
+    vg_ref, block_ref, first_ref, out_ref, act_v,
     vt, a_buf, r_buf, x1, s1, x2, near_out, near_in, far_out, far_in, g_buf, g_in, rows, denom,
-    bias_out, bias_x, bias_n, bias_f,
+    bias_out, bias_x, bias_n, bias_f, z_out, z_in, in_sem, act_sem, z_send, z_recv, greet_a, greet_b,
     v_send, v_recv, w_send, a_send, a_recv, x1_send, x1_recv, x2_send, x2_recv,
     n_send, n_recv, f_send, f_recv, g_send, g_recv, b_send, b_recv,
 ):
@@ -67,6 +63,7 @@
     mp_others = [(mp + k) % NMP for k in range(1, NMP)]
     y_others = [(y + k) % NY for k in range(1, NY)]
     x_others = [(x + k) % NX for k in range(1, NX)]
+    z_others = [(z + k) % NZ for k in range(1, NZ)]
     zl_others = [(zl + k) % 4 for k in range(1, 4)]
     zh_others = [(zh + k) % 4 for k in range(1, 4)]
     before, after = (dp + NDP - 1) % NDP, (dp + 1) % NDP
@@ -80,12 +77,17 @@
     def pair_of(v):
         return v + 1 - 2 * (v % 2)
 
+    load = [
+        pltpu.make_async_copy(src, dst, in_sem.at[k])
+        for k, (src, dst) in enumerate([(vg_hbm, vg_ref), (block_hbm, block_ref), (first_hbm.at[:, 0], first_ref)])
+    ]
     with jax.named_scope("entry"):
+        for copy in load:
+            copy.start()
         barrier = pltpu.get_barrier_semaphore()
         partners = [at(m=m) for m in mp_others]
         partners += [at(px=v) for v in x_others]
-        partners += [at(pz=zh * 4 + v) for v in zl_others]
-        partners += [at(pz=v * 4 + zl) for v in zh_others]
+        partners += [at(pz=(z + k) % NZ) for k in (1, 2, 3, 13, 14, 15)]
         partners += [at(p=p, m=m) for p in (before, after) for m in range(NMP)]
         for partner in partners:
             pl.semaphore_signal(barrier, inc=1, device_id=partner, device_id_type=MESH)
@@ -93,45 +95,69 @@
             columns = pl.ds(pl.multiple_of(mp * SLICE + j * LANES, LANES), LANES)
             own = pl.ds(pl.multiple_of(mp * TOK, TOK), TOK)
             pltpu.make_async_copy(act_ref.at[:, columns], a_buf.at[j, own], a_recv.at[j]).start()
+            for m in range(NMP):
+                columns = pl.ds(m * SLICE + j * LANES, LANES)
+                pltpu.make_async_copy(act_ref.at[:, columns], act_v.at[j, m], act_sem.at[j]).start()
     with jax.named_scope("turn"):
+        load[0].wait()
         vt[mp] = lax.dot_general(
-            perm_ref[...], vg_ref[...], (((1,), (1,)), ((), ())), preferred_element_type=jnp.float32
+            unit_order(), vg_ref[...], (((1,), (1,)), ((), ())), preferred_element_type=jnp.float32
         ).astype(jnp.bfloat16)
         bias = jnp.sum(vg_ref[...].astype(jnp.float32), axis=0, keepdims=True)
         bias_out[0] = jnp.broadcast_to(bias, (8, LANES))
     with jax.named_scope("barrier"):
         pl.semaphore_wait(barrier, len(partners))
 
-    def v_copy(v, slot):
-        return remote(vt.at[slot], vt.at[slot], v_send, v_recv.at[slot], at(m=v * NC + c))
-
-    def w_copy(slot):
-        return remote(vt.at[slot], vt.at[slot], w_send, v_recv.at[slot], at(m=y * NC + 1 - c))
+    up, down, across = y_others[0], y_others[2], y_others[1]
+
+    def v_copy(v, slot, part):
+        ref = vt.at[slot, pl.ds(part * 64, 64)]
+        return remote(ref, ref, v_send, v_recv.at[slot, part], at(m=v * NC + c))
+
+    def w_copy(slot, part):
+        ref = vt.at[slot, pl.ds(part * 64, 64)]
+        return remote(ref, ref, w_send, v_recv.at[slot, part], at(m=y * NC + 1 - c))
 
     def a_copy(j, m):
-        columns = pl.ds(pl.multiple_of(m * SLICE + j * LANES, LANES), LANES)
         own = pl.ds(pl.multiple_of(mp * TOK, TOK), TOK)
-        return remote(act_ref.at[:, columns], a_buf.at[j, own], a_send.at[j], a_recv.at[j], at(m=m))
-
+        return remote(act_v.at[j, m], a_buf.at[j, own], a_send.at[j], a_recv.at[j], at(m=m))
+
+    def greet(sem, k):
+        for to in (k, NZ - k):
+            pl.semaphore_signal(sem, inc=1, device_id=at(pz=(z + to) % NZ), device_id_type=MESH)
+
+    greet(greet_a, 3)
     with jax.named_scope("send"):
-        for v in y_others:
-            v_copy(v, mp).start()
-        w_copy(mp).start()
         for j in range(CH):
-            for m in mp_others:
-                a_copy(j, m).start()
+            pltpu.make_async_copy(act_v.at[j], act_v.at[j], act_sem.at[j]).wait()
+        for part in range(2):
+            v_copy(up, mp, part).start()
+            v_copy(down, mp, 1 - part).start()
+        for part in range(2):
+            w_copy(mp, part).start()
+        for m in mp_others:
+            a_copy(0, m).start()
 
         @pl.when(x != 0)
         def _():
             remote(bias_out.at[0], bias_x.at[x], b_send.at[0], b_recv.at[0], at(px=0)).start()
 
     with jax.named_scope("forward"):
-        for v in y_others:
-            slot = v * NC + c
-            v_copy(y, slot).wait_recv()
-            w_copy(slot).start()
+        from_down, from_up, opposite = down * NC + c, up * NC + c, across * NC + c
+        for slot, part, to in ((from_down, 0, up), (from_up, 1, down)):
+            w_copy(slot, part).wait_recv()
+            v_copy(to, slot, part).start()
+            w_copy(slot, part).start()
+        for m in mp_others:
+            a_copy(1, m).start()
+        pl.semaphore_wait(greet_a, 2)
+        greet(greet_b, 6)
+        for slot, part in ((from_down, 1), (from_up, 0), (opposite, 0), (opposite, 1)):
+            w_copy(slot, part).wait_recv()
+            w_copy(slot, part).start()
         for v in range(NY):
-            w_copy(v * NC + 1 - c).wait_recv()
+            for part in range(2):
+                w_copy(v * NC + 1 - c, part).wait_recv()
 
     def first_of(half):
         return (pair, cross_of(pair)) if half == 0 else (cross, pair_of(cross))
@@ -158,9 +184,15 @@
     def far_copy(j, v):
         return remote(far_out.at[j, v], far_in.at[j, zh], f_send.at[j], f_recv.at[j], at(pz=v * 4 + zl))
 
+    def z_copy(v):
+        return remote(z_out.at[v], z_in.at[z], z_send, z_recv, at(pz=v))
+
     def stage_mul(j):
         with jax.named_scope("mul"):
             pltpu.make_async_copy(a_buf.at[j], a_buf.at[j], a_recv.at[j]).wait()
+            if j + 2 < CH:
+                for m in mp_others:
+                    a_copy(j + 2, m).start()
             for half in range(2):
                 for v in range(NY):
                     res = jnp.dot(vt[v * NC + half], a_buf[j], preferred_element_type=jnp.float32)
@@ -185,10 +217,19 @@
                 x2_copy(j, half).wait_recv()
                 total = r_buf[j, half, block(x)] + x1[j, half, 0] + x2[j, half]
                 for v in range(4):
-                    near_out[j, v, half * 32 : half * 32 + 32] = total[v * 32 : v * 32 + 32]
-            for v in zl_others:
-                near_copy(j, v).start()
-            near_in[j, zl] = near_out[j, zl]
+                    if j < CH - 1:
+                        near_out[j, v, half * 32 : half * 32 + 32] = total[v * 32 : v * 32 + 32]
+                    else:
+                        for w in range(4):
+                            z_out[w * 4 + v, half * 8 : half * 8 + 8] = total[v * 32 + w * 8 : v * 32 + w * 8 + 8]
+            if j < CH - 1:
+                for v in zl_others:
+                    near_copy(j, v).start()
+                near_in[j, zl] = near_out[j, zl]
+            else:
+                for v in z_others:
+                    z_copy(v).start()
+                z_in[z] = z_out[z]
 
     def stage_near(j):
         with jax.named_scope("near"):
@@ -205,8 +246,16 @@
         with jax.named_scope("far"):
             pltpu.make_async_copy(far_in.at[j, pl.ds(0, 3)], far_in.at[j, pl.ds(0, 3)], f_recv.at[j]).wait()
             total = far_in[j, 0] + far_in[j, 1] + far_in[j, 2] + far_in[j, 3]
-            for half in range(2):
-                g_buf[pl.ds(half * 64 + j, 8, stride=8), :] = total[half * 8 : half * 8 + 8]
+            keep(j, total)
+
+    def stage_z(j):
+        with jax.named_scope("z"):
+            pltpu.make_async_copy(z_in.at[pl.ds(0, 15)], z_in.at[pl.ds(0, 15)], z_recv).wait()
+            keep(j, functools.reduce(jnp.add, [z_in[v] for v in range(NZ)]))
+
+    def keep(j, total):
+        for half in range(2):
+            g_buf[pl.ds(half * 64 + j, 8, stride=8), :] = total[half * 8 : half * 8 + 8]
 
     def bias_stage(k):
         if k == 0:
@@ -239,13 +288,19 @@
                 rows[0:8] = bias_out[2] + bias_f[1] + bias_f[2] + bias_f[3]
 
     rows[0:8] = jnp.zeros((8, LANES), jnp.float32)
-    stages = [stage_mul, stage_x1, stage_x2, stage_near, stage_far]
-    for step in range(CH + len(stages) - 1):
-        for lag, stage in enumerate(stages):
-            if 0 <= step - lag < CH:
+    lags = [(stage_mul, 0), (stage_x1, 1), (stage_x2, 2), (stage_near, 4)]
+    for step in range(CH + 3):
+        for stage, lag in lags:
+            if 0 <= step - lag < (CH - 1 if stage is stage_near else CH):
                 stage(step - lag)
-        if step < 3:
-            bias_stage(step)
+        if step in (1, 3):
+            bias_stage(step // 2)
+        if step == 2:
+            pl.semaphore_wait(greet_b, 2)
+    bias_stage(2)
+    for j in range(CH - 1):
+        stage_far(j)
+    stage_z(CH - 1)
 
     def g_copy(k, m):
         src = g_buf.at[pl.ds(pl.multiple_of(((m % NC) * NY + m // NC) * 16, 16), 16)]
@@ -263,6 +318,8 @@
         pltpu.make_async_copy(g_in.at[1], g_in.at[1], g_recv.at[1]).wait()
 
     with jax.named_scope("update"):
+        load[1].wait()
+        load[2].wait()
         for k in range(2):
             for m in range(NMP):
                 for e in range(2):
@@ -279,16 +336,23 @@
             denom[8 + k * 40 : 48 + k * 40] = jnp.full((40, LANES), unit_moment, jnp.float32)
         grad = rows[pl.ds(dp + 7, ROWS_P), :]
         moment = denom[pl.ds(dp + 7, ROWS_P), :]
-        momentum = beta_one * first_ref[0] + (1.0 - beta_one) * grad
+        momentum = beta_one * first_ref[...] + (1.0 - beta_one) * grad
         step_dir = momentum / bias_one / (jnp.sqrt(moment / bias_two) + epsilon)
         position = dp * ROWS_P + lax.broadcasted_iota(jnp.int32, (ROWS_P, LANES), 0)
-        out_ref[0] = jnp.where(position < USED_ROWS, step_dir, 0.0)
+        out_ref[...] = jnp.where(position < USED_ROWS, step_dir, 0.0)
+        store = pltpu.make_async_copy(out_ref, out_hbm.at[:, 0], in_sem.at[3])
+        store.start()
 
     with jax.named_scope("drain"):
-        for v in y_others:
-            v_copy(v, mp).wait_send()
+        store.wait()
+        for part in range(2):
+            v_copy(up, mp, part).wait_send()
+            v_copy(down, mp, part).wait_send()
+        v_copy(up, from_down, 0).wait_send()
+        v_copy(down, from_up, 1).wait_send()
         for v in range(NY):
-            w_copy(v * NC + c).wait_send()
+            for part in range(2):
+                w_copy(v * NC + c, part).wait_send()
         for j in range(CH):
             for m in mp_others:
                 a_copy(j, m).wait_send()
@@ -296,10 +360,13 @@
                 for copy in x1_copies(j, half):
                     copy.wait_send()
                 x2_copy(j, half).wait_send()
+        for j in range(CH - 1):
             for v in zl_others:
                 near_copy(j, v).wait_send()
             for v in zh_others:
                 far_copy(j, v).wait_send()
+        for v in z_others:
+            z_copy(v).wait_send()
         for m in mp_others:
             g_copy(0, m).wait_send()
         for m in range(NMP):
@@ -321,19 +388,17 @@
 def body(value_grads, activations, block_moment, first_moment):
     f32, bf16 = jnp.float32, jnp.bfloat16
     dma = pltpu.SemaphoreType.DMA
-    vmem = pl.BlockSpec(memory_space=pltpu.VMEM)
-    return pl.pallas_call(
+    update = pl.pallas_call(
         kernel,
-        out_shape=jax.ShapeDtypeStruct(first_moment.shape, f32),
-        in_specs=[
-            vmem,
-            vmem,
-            pl.BlockSpec(memory_space=pl.ANY),
-            pl.BlockSpec(memory_space=pltpu.SMEM),
-            vmem,
-        ],
-        out_specs=vmem,
+        out_shape=jax.ShapeDtypeStruct((ROWS_P, 1, LANES), f32),
+        in_specs=[pl.BlockSpec(memory_space=pltpu.HBM)] * 4,
+        out_specs=pl.BlockSpec(memory_space=pltpu.HBM),
         scratch_shapes=[
+            pltpu.VMEM(value_grads.shape, bf16),
+            pltpu.SMEM(block_moment.shape, f32),
+            pltpu.VMEM((ROWS_P, LANES), f32),
+            pltpu.VMEM((ROWS_P, LANES), f32),
+            pltpu.VMEM((CH, NMP, TOK, LANES), bf16),
             pltpu.VMEM((NMP, HEAD, TOKENS), bf16),
             pltpu.VMEM((CH, TOKENS, LANES), bf16),
             pltpu.VMEM((CH, 2, 512, LANES), f32),
@@ -352,16 +417,21 @@
             pltpu.VMEM((4, 8, LANES), f32),
             pltpu.VMEM((4, 8, LANES), f32),
             pltpu.VMEM((4, 8, LANES), f32),
-            dma, dma((NMP,)), dma, dma((CH,)), dma((CH,)),
+            pltpu.VMEM((NZ, 16, LANES), f32),
+            pltpu.VMEM((NZ, 16, LANES), f32),
+            dma((4,)), dma((CH,)), dma, dma,
+            pltpu.SemaphoreType.REGULAR, pltpu.SemaphoreType.REGULAR,
+            dma, dma((NMP, 2)), dma, dma((CH,)), dma((CH,)),
             dma((CH, 2)), dma((CH, 2, 2)), dma((CH, 2)), dma((CH, 2)),
             dma((CH,)), dma((CH,)), dma((CH,)), dma((CH,)),
             dma, dma((2,)), dma((3,)), dma((3,)),
         ],
         compiler_params=pltpu.CompilerParams(
-            collective_id=0, has_side_effects=True, vmem_limit_bytes=48 << 20
+            collective_id=0, has_side_effects=True, vmem_limit_bytes=63 << 20
         ),
         name="gradient_step",
-    )(jnp.asarray(unit_order(), bf16), value_grads, activations, block_moment, first_moment)
+    )(value_grads, activations, block_moment, first_moment.reshape(ROWS_P, 1, LANES))
+    return update.reshape(first_moment.shape)
 
 
 def solution(mesh):

time: 89.6 us -> 81 us (0.904)
  Pallas kernels: 84.1 us -> 79.4 us
  local copies, waits for them, and re-layouts: 5.23 us -> 1.4 us
    pallas_call x1, Pallas kernels: 84.1 us -> 79.4 us  [body(): pl.pallas_call(kernel, out_shape=jax.ShapeDtypeStruct((ROWS_P, 1, LANES),...]
    unnamed x9 -> x1, local copies, waits for them, and re-layouts: 4.57 us -> 1.4 us
where the time goes in v2:
time: 81 us; the launch traced here: 80.8 us
  Pallas kernels  79.4 us (98%)
  local copies, waits for them, and re-layouts  1.4 us (2%)
    pallas_call x1, Pallas kernels, body(): pl.pallas_call(kernel, out_shape=jax.ShapeDtypeStruct((ROWS_P, 1, LANES),...  79.4 us

profile of v2, /device:TPU:1, one launch (start us, length us, event | category | flops | bytes accessed | tf_op | source)
XLA Modules:
  0.0 80.8 jit_solution(6849267871022977331)
XLA Ops:
  0.0 79.4 %gradient_step.1 = f32[81,1,128]{2,1,0:T(1,128)} custom-call(bf16[1152,128]{1,0:T(8,128)(2,1)} %vg_hbm.1, bf16[144,5120]{1,0:T(8,128)(2,1)} %act_ref.1, f32[1032]{0:T(1024)} %block_hbm.1, f32[81,1,128]{2,1,0:T(1,128)} %bitcast.3), custom_call_target="tpu_custom_call" | custom-call | tf_op jit(solution)/shard_map/gradient_step/pallas_call | solution.py:391
  79.4 1.4 %copy.6 = f32[1,81,128]{2,0,1:T(1,128)} copy(f32[1,81,128]{2,0,1:T(1,128)} %bitcast.2) | data formatting | bytes 82944

commit v3 on v2

--- a/solution.py
+++ b/solution.py
@@ -24,9 +24,13 @@
 WIDTH = 5120
 SLICE = WIDTH // NMP
 CH = SLICE // LANES
+STEPS = CH - 1
 ROWS_P = 81
 USED_ROWS = 1 + HEAD * WIDTH // LANES
 UNIT_ROWS = WIDTH // LANES
+
+
+FAR_FIRST = sorted(range(1, NZ), key=lambda k: -min(k, NZ - k))
 
 
 def unit_order():
@@ -60,12 +64,12 @@
             src_ref=src, dst_ref=dst, send_sem=send, recv_sem=recv, device_id=device, device_id_type=MESH
         )
 
-    mp_others = [(mp + k) % NMP for k in range(1, NMP)]
+    mp_others = [(mp + k) % NMP for k in (4, 3, 5, 2, 6, 1, 7)]
     y_others = [(y + k) % NY for k in range(1, NY)]
     x_others = [(x + k) % NX for k in range(1, NX)]
-    z_others = [(z + k) % NZ for k in range(1, NZ)]
+    z_others = [(z + k) % NZ for k in FAR_FIRST]
     zl_others = [(zl + k) % 4 for k in range(1, 4)]
-    zh_others = [(zh + k) % 4 for k in range(1, 4)]
+    zh_others = [(zh + k) % 4 for k in (2, 1, 3)]
     before, after = (dp + NDP - 1) % NDP, (dp + 1) % NDP
     odd = x % 2
     pair = x + 1 - 2 * odd
@@ -81,6 +85,19 @@
         pltpu.make_async_copy(src, dst, in_sem.at[k])
         for k, (src, dst) in enumerate([(vg_hbm, vg_ref), (block_hbm, block_ref), (first_hbm.at[:, 0], first_ref)])
     ]
+    def load_chunk(j):
+        columns = pl.ds(pl.multiple_of(mp * SLICE + j * LANES, LANES), LANES)
+        own = pl.ds(pl.multiple_of(mp * TOK, TOK), TOK)
+        pltpu.make_async_copy(act_ref.at[:, columns], a_buf.at[j, own], a_recv.at[j]).start()
+        for m in range(NMP):
+            columns = pl.ds(m * SLICE + j * LANES, LANES)
+            pltpu.make_async_copy(act_ref.at[:, columns], act_v.at[j, m], act_sem.at[j]).start()
+
+    def send_chunk(j):
+        pltpu.make_async_copy(act_v.at[j], act_v.at[j], act_sem.at[j]).wait()
+        for m in mp_others:
+            a_copy(j, m).start()
+
     with jax.named_scope("entry"):
         for copy in load:
             copy.start()
@@ -91,13 +108,7 @@
         partners += [at(p=p, m=m) for p in (before, after) for m in range(NMP)]
         for partner in partners:
             pl.semaphore_signal(barrier, inc=1, device_id=partner, device_id_type=MESH)
-        for j in range(CH):
-            columns = pl.ds(pl.multiple_of(mp * SLICE + j * LANES, LANES), LANES)
-            own = pl.ds(pl.multiple_of(mp * TOK, TOK), TOK)
-            pltpu.make_async_copy(act_ref.at[:, columns], a_buf.at[j, own], a_recv.at[j]).start()
-            for m in range(NMP):
-                columns = pl.ds(m * SLICE + j * LANES, LANES)
-                pltpu.make_async_copy(act_ref.at[:, columns], act_v.at[j, m], act_sem.at[j]).start()
+        load_chunk(0)
     with jax.named_scope("turn"):
         load[0].wait()
         vt[mp] = lax.dot_general(
@@ -126,17 +137,16 @@
         for to in (k, NZ - k):
             pl.semaphore_signal(sem, inc=1, device_id=at(pz=(z + to) % NZ), device_id_type=MESH)
 
-    greet(greet_a, 3)
     with jax.named_scope("send"):
-        for j in range(CH):
-            pltpu.make_async_copy(act_v.at[j], act_v.at[j], act_sem.at[j]).wait()
         for part in range(2):
             v_copy(up, mp, part).start()
             v_copy(down, mp, 1 - part).start()
         for part in range(2):
             w_copy(mp, part).start()
-        for m in mp_others:
-            a_copy(0, m).start()
+        send_chunk(0)
+        greet(greet_a, 3)
+        for j in range(1, CH):
+            load_chunk(j)
 
         @pl.when(x != 0)
         def _():
@@ -148,8 +158,7 @@
             w_copy(slot, part).wait_recv()
             v_copy(to, slot, part).start()
             w_copy(slot, part).start()
-        for m in mp_others:
-            a_copy(1, m).start()
+        send_chunk(1)
         pl.semaphore_wait(greet_a, 2)
         greet(greet_b, 6)
         for slot, part in ((from_down, 1), (from_up, 0), (opposite, 0), (opposite, 1)):
@@ -184,15 +193,14 @@
     def far_copy(j, v):
         return remote(far_out.at[j, v], far_in.at[j, zh], f_send.at[j], f_recv.at[j], at(pz=v * 4 + zl))
 
-    def z_copy(v):
-        return remote(z_out.at[v], z_in.at[z], z_send, z_recv, at(pz=v))
+    def z_copy(j, v):
+        return remote(z_out.at[j - STEPS, v], z_in.at[j - STEPS, z], z_send.at[j - STEPS], z_recv.at[j - STEPS], at(pz=v))
 
     def stage_mul(j):
         with jax.named_scope("mul"):
             pltpu.make_async_copy(a_buf.at[j], a_buf.at[j], a_recv.at[j]).wait()
             if j + 2 < CH:
-                for m in mp_others:
-                    a_copy(j + 2, m).start()
+                send_chunk(j + 2)
             for half in range(2):
                 for v in range(NY):
                     res = jnp.dot(vt[v * NC + half], a_buf[j], preferred_element_type=jnp.float32)
@@ -217,19 +225,19 @@
                 x2_copy(j, half).wait_recv()
                 total = r_buf[j, half, block(x)] + x1[j, half, 0] + x2[j, half]
                 for v in range(4):
-                    if j < CH - 1:
+                    if j < STEPS:
                         near_out[j, v, half * 32 : half * 32 + 32] = total[v * 32 : v * 32 + 32]
                     else:
                         for w in range(4):
-                            z_out[w * 4 + v, half * 8 : half * 8 + 8] = total[v * 32 + w * 8 : v * 32 + w * 8 + 8]
-            if j < CH - 1:
+                            z_out[j - STEPS, w * 4 + v, half * 8 : half * 8 + 8] = total[v * 32 + w * 8 : v * 32 + w * 8 + 8]
+            if j < STEPS:
                 for v in zl_others:
                     near_copy(j, v).start()
                 near_in[j, zl] = near_out[j, zl]
             else:
                 for v in z_others:
-                    z_copy(v).start()
-                z_in[z] = z_out[z]
+                    z_copy(j, v).start()
+                z_in[j - STEPS, z] = z_out[j - STEPS, z]
 
     def stage_near(j):
         with jax.named_scope("near"):
@@ -250,8 +258,9 @@
 
     def stage_z(j):
         with jax.named_scope("z"):
-            pltpu.make_async_copy(z_in.at[pl.ds(0, 15)], z_in.at[pl.ds(0, 15)], z_recv).wait()
-            keep(j, functools.reduce(jnp.add, [z_in[v] for v in range(NZ)]))
+            got = z_in.at[j - STEPS, pl.ds(0, NZ - 1)]
+            pltpu.make_async_copy(got, got, z_recv.at[j - STEPS]).wait()
+            keep(j, functools.reduce(jnp.add, [z_in[j - STEPS, v] for v in range(NZ)]))
 
     def keep(j, total):
         for half in range(2):
@@ -288,19 +297,20 @@
                 rows[0:8] = bias_out[2] + bias_f[1] + bias_f[2] + bias_f[3]
 
     rows[0:8] = jnp.zeros((8, LANES), jnp.float32)
-    lags = [(stage_mul, 0), (stage_x1, 1), (stage_x2, 2), (stage_near, 4)]
+    lags = [(stage_mul, 0), (stage_x1, 1), (stage_x2, 2), (stage_near, 3)]
     for step in range(CH + 3):
         for stage, lag in lags:
-            if 0 <= step - lag < (CH - 1 if stage is stage_near else CH):
+            if 0 <= step - lag < (STEPS if stage is stage_near else CH):
                 stage(step - lag)
         if step in (1, 3):
             bias_stage(step // 2)
         if step == 2:
             pl.semaphore_wait(greet_b, 2)
     bias_stage(2)
-    for j in range(CH - 1):
+    for j in range(STEPS):
         stage_far(j)
-    stage_z(CH - 1)
+    for j in range(STEPS, CH):
+        stage_z(j)
 
     def g_copy(k, m):
         src = g_buf.at[pl.ds(pl.multiple_of(((m % NC) * NY + m // NC) * 16, 16), 16)]
@@ -308,10 +318,10 @@
         return remote(src, dst, g_send, g_recv.at[k], at(p=dp if k == 0 else before, m=m))
 
     with jax.named_scope("heads"):
+        for m in mp_others + [mp]:
+            g_copy(1, m).start()
         for m in mp_others:
             g_copy(0, m).start()
-        for k in range(NMP):
-            g_copy(1, (mp + k) % NMP).start()
         own = pl.ds(pl.multiple_of(mp * 16, 16), 16)
         g_in[0, own] = g_buf[pl.ds(pl.multiple_of((c * NY + y) * 16, 16), 16)]
         pltpu.make_async_copy(g_in.at[0, pl.ds(0, 112)], g_in.at[0, pl.ds(0, 112)], g_recv.at[0]).wait()
@@ -360,13 +370,14 @@
                 for copy in x1_copies(j, half):
                     copy.wait_send()
                 x2_copy(j, half).wait_send()
-        for j in range(CH - 1):
+        for j in range(STEPS):
             for v in zl_others:
                 near_copy(j, v).wait_send()
             for v in zh_others:
                 far_copy(j, v).wait_send()
-        for v in z_others:
-            z_copy(v).wait_send()
+        for j in range(STEPS, CH):
+            for v in z_others:
+                z_copy(j, v).wait_send()
         for m in mp_others:
             g_copy(0, m).wait_send()
         for m in range(NMP):
@@ -417,9 +428,9 @@
             pltpu.VMEM((4, 8, LANES), f32),
             pltpu.VMEM((4, 8, LANES), f32),
             pltpu.VMEM((4, 8, LANES), f32),
-            pltpu.VMEM((NZ, 16, LANES), f32),
-            pltpu.VMEM((NZ, 16, LANES), f32),
-            dma((4,)), dma((CH,)), dma, dma,
+            pltpu.VMEM((CH - STEPS, NZ, 16, LANES), f32),
+            pltpu.VMEM((CH - STEPS, NZ, 16, LANES), f32),
+            dma((4,)), dma((CH,)), dma((CH - STEPS,)), dma((CH - STEPS,)),
             pltpu.SemaphoreType.REGULAR, pltpu.SemaphoreType.REGULAR,
             dma, dma((NMP, 2)), dma, dma((CH,)), dma((CH,)),
             dma((CH, 2)), dma((CH, 2, 2)), dma((CH, 2)), dma((CH, 2)),

time: 81 us -> 79.3 us (0.979)
  Pallas kernels: 79.4 us -> 77.7 us
    pallas_call x1, Pallas kernels: 79.4 us -> 77.7 us  [body(): pl.pallas_call(kernel, out_shape=jax.ShapeDtypeStruct((ROWS_P, 1, LANES),...]
where the time goes in v3:
time: 79.3 us; the launch traced here: 79.2 us
  Pallas kernels  77.7 us (98%)
  local copies, waits for them, and re-layouts  1.4 us (2%)
    pallas_call x1, Pallas kernels, body(): pl.pallas_call(kernel, out_shape=jax.ShapeDtypeStruct((ROWS_P, 1, LANES),...  77.7 us

profile of v3, /device:TPU:1, one launch (start us, length us, event | category | flops | bytes accessed | tf_op | source)
XLA Modules:
  0.0 79.2 jit_solution(7825360838094098111)
XLA Ops:
  0.0 77.7 %gradient_step.1 = f32[81,1,128]{2,1,0:T(1,128)} custom-call(bf16[1152,128]{1,0:T(8,128)(2,1)} %vg_hbm.1, bf16[144,5120]{1,0:T(8,128)(2,1)} %act_ref.1, f32[1032]{0:T(1024)} %block_hbm.1, f32[81,1,128]{2,1,0:T(1,128)} %bitcast.3), custom_call_target="tpu_custom_call" | custom-call | tf_op jit(solution)/shard_map/gradient_step/pallas_call | solution.py:402
  77.7 1.4 %copy.6 = f32[1,81,128]{2,0,1:T(1,128)} copy(f32[1,81,128]{2,0,1:T(1,128)} %bitcast.2) | data formatting | bytes 82944

commit v4 on v3

--- a/solution.py
+++ b/solution.py
@@ -114,8 +114,6 @@
         vt[mp] = lax.dot_general(
             unit_order(), vg_ref[...], (((1,), (1,)), ((), ())), preferred_element_type=jnp.float32
         ).astype(jnp.bfloat16)
-        bias = jnp.sum(vg_ref[...].astype(jnp.float32), axis=0, keepdims=True)
-        bias_out[0] = jnp.broadcast_to(bias, (8, LANES))
     with jax.named_scope("barrier"):
         pl.semaphore_wait(barrier, len(partners))
 
@@ -147,6 +145,9 @@
         greet(greet_a, 3)
         for j in range(1, CH):
             load_chunk(j)
+
+        bias = jnp.sum(vg_ref[...].astype(jnp.float32), axis=0, keepdims=True)
+        bias_out[0] = jnp.broadcast_to(bias, (8, LANES))
 
         @pl.when(x != 0)
         def _():
@@ -193,8 +194,9 @@
     def far_copy(j, v):
         return remote(far_out.at[j, v], far_in.at[j, zh], f_send.at[j], f_recv.at[j], at(pz=v * 4 + zl))
 
-    def z_copy(j, v):
-        return remote(z_out.at[j - STEPS, v], z_in.at[j - STEPS, z], z_send.at[j - STEPS], z_recv.at[j - STEPS], at(pz=v))
+    def z_copy(j, half, v):
+        k, part = j - STEPS, pl.ds(half * 8, 8)
+        return remote(z_out.at[k, v, part], z_in.at[k, z, part], z_send.at[k], z_recv.at[k], at(pz=v))
 
     def stage_mul(j):
         with jax.named_scope("mul"):
@@ -230,13 +232,14 @@
                     else:
                         for w in range(4):
                             z_out[j - STEPS, w * 4 + v, half * 8 : half * 8 + 8] = total[v * 32 + w * 8 : v * 32 + w * 8 + 8]
+                if j >= STEPS:
+                    for v in z_others:
+                        z_copy(j, half, v).start()
             if j < STEPS:
                 for v in zl_others:
                     near_copy(j, v).start()
                 near_in[j, zl] = near_out[j, zl]
             else:
-                for v in z_others:
-                    z_copy(j, v).start()
                 z_in[j - STEPS, z] = z_out[j - STEPS, z]
 
     def stage_near(j):
@@ -307,6 +310,22 @@
         if step == 2:
             pl.semaphore_wait(greet_b, 2)
     bias_stage(2)
+    with jax.named_scope("sent"):
+        for part in range(2):
+            v_copy(up, mp, part).wait_send()
+            v_copy(down, mp, part).wait_send()
+        v_copy(up, from_down, 0).wait_send()
+        v_copy(down, from_up, 1).wait_send()
+        for v in range(NY):
+            for part in range(2):
+                w_copy(v * NC + c, part).wait_send()
+        for j in range(CH):
+            for m in mp_others:
+                a_copy(j, m).wait_send()
+            for half in range(2):
+                for copy in x1_copies(j, half):
+                    copy.wait_send()
+                x2_copy(j, half).wait_send()
     for j in range(STEPS):
         stage_far(j)
     for j in range(STEPS, CH):
@@ -355,21 +374,6 @@
 
     with jax.named_scope("drain"):
         store.wait()
-        for part in range(2):
-            v_copy(up, mp, part).wait_send()
-            v_copy(down, mp, part).wait_send()
-        v_copy(up, from_down, 0).wait_send()
-        v_copy(down, from_up, 1).wait_send()
-        for v in range(NY):
-            for part in range(2):
-                w_copy(v * NC + c, part).wait_send()
-        for j in range(CH):
-            for m in mp_others:
-                a_copy(j, m).wait_send()
-            for half in range(2):
-                for copy in x1_copies(j, half):
-                    copy.wait_send()
-                x2_copy(j, half).wait_send()
         for j in range(STEPS):
             for v in zl_others:
                 near_copy(j, v).wait_send()
@@ -377,7 +381,8 @@
                 far_copy(j, v).wait_send()
         for j in range(STEPS, CH):
             for v in z_others:
-                z_copy(j, v).wait_send()
+                for half in range(2):
+                    z_copy(j, half, v).wait_send()
         for m in mp_others:
             g_copy(0, m).wait_send()
         for m in range(NMP):

time: 79.3 us -> 79.1 us (level)
  no operation moved by 1% of the time
where the time goes in v4:
time: 79.1 us; the launch traced here: 78.9 us
  Pallas kernels  77.5 us (98%)
  local copies, waits for them, and re-layouts  1.4 us (2%)
    pallas_call x1, Pallas kernels, body(): pl.pallas_call(kernel, out_shape=jax.ShapeDtypeStruct((ROWS_P, 1, LANES),...  77.5 us

profile of v4, /device:TPU:1, one launch (start us, length us, event | category | flops | bytes accessed | tf_op | source)
XLA Modules:
  0.0 78.9 jit_solution(2966821885869533420)
XLA Ops:
  0.0 77.5 %gradient_step.1 = f32[81,1,128]{2,1,0:T(1,128)} custom-call(bf16[1152,128]{1,0:T(8,128)(2,1)} %vg_hbm.1, bf16[144,5120]{1,0:T(8,128)(2,1)} %act_ref.1, f32[1032]{0:T(1024)} %block_hbm.1, f32[81,1,128]{2,1,0:T(1,128)} %bitcast.3), custom_call_target="tpu_custom_call" | custom-call | tf_op jit(solution)/shard_map/gradient_step/pallas_call | solution.py:407
  77.5 1.4 %copy.6 = f32[1,81,128]{2,0,1:T(1,128)} copy(f32[1,81,128]{2,0,1:T(1,128)} %bitcast.2) | data formatting | bytes 82944

commit v5 on v4

--- a/solution.py
+++ b/solution.py
@@ -302,6 +302,8 @@
     rows[0:8] = jnp.zeros((8, LANES), jnp.float32)
     lags = [(stage_mul, 0), (stage_x1, 1), (stage_x2, 2), (stage_near, 3)]
     for step in range(CH + 3):
+        if step == CH + 1:
+            lags = [lags[3], lags[2]]
         for stage, lag in lags:
             if 0 <= step - lag < (STEPS if stage is stage_near else CH):
                 stage(step - lag)

time: 79.1 us -> 80.4 us (1.016)
  Pallas kernels: 77.5 us -> 78.8 us
    pallas_call x1, Pallas kernels: 77.5 us -> 78.8 us  [body(): pl.pallas_call(kernel, out_shape=jax.ShapeDtypeStruct((ROWS_P, 1, LANES),...]
where the time goes in v5:
time: 80.4 us; the launch traced here: 80.2 us
  Pallas kernels  78.8 us (98%)
  local copies, waits for them, and re-layouts  1.4 us (2%)
    pallas_call x1, Pallas kernels, body(): pl.pallas_call(kernel, out_shape=jax.ShapeDtypeStruct((ROWS_P, 1, LANES),...  78.8 us

profile of v5, /device:TPU:1, one launch (start us, length us, event | category | flops | bytes accessed | tf_op | source)
XLA Modules:
  0.0 80.2 jit_solution(6079368845663443199)
XLA Ops:
  0.0 78.8 %gradient_step.1 = f32[81,1,128]{2,1,0:T(1,128)} custom-call(bf16[1152,128]{1,0:T(8,128)(2,1)} %vg_hbm.1, bf16[144,5120]{1,0:T(8,128)(2,1)} %act_ref.1, f32[1032]{0:T(1024)} %block_hbm.1, f32[81,1,128]{2,1,0:T(1,128)} %bitcast.3), custom_call_target="tpu_custom_call" | custom-call | tf_op jit(solution)/shard_map/gradient_step/pallas_call | solution.py:409
  78.8 1.4 %copy.6 = f32[1,81,128]{2,0,1:T(1,128)} copy(f32[1,81,128]{2,0,1:T(1,128)} %bitcast.2) | data formatting | bytes 82944
